TPU v7x, 32 devices: a whole 2x2x4 slice. The times are simulated.
32 devices in a mesh: layer: 4 (over z), prow: 2 (over y), pcol: 4 (over x, core).
Axes of the slice: x: 2, y: 2, z: 4, core: 2. Of those that a mesh axis runs over, the one named last changes fastest.
Arguments:
- front: bfloat16 [3072, 3072], P('prow', 'pcol')
- lower_desc: bfloat16 [3072, 2048], P('prow', 'layer')
- upper_desc: bfloat16 [2048, 3072], P('layer', 'pcol')
- pattern: int32 [4, 32], P('layer'), may hold values 0 or 1
- pivot: int32 [16, 192], P('prow'), may hold values from 0 to 191, as said below
Outputs:
- factored: float32 [3072, 3072], P('prow', 'pcol')
Inputs may be any that keep to these rules, and one draw needn't show every extreme that they name: Each row of pivot lists every offset 0 to 191 once.
All inputs are finite; a program needn't handle non-finite values. No bound on the sum of `pattern` on one device may be relied on, other than what follows from the above.
Results may differ from a plain program's by a relative error of at most 0.0003.
Values sent between devices are 32-bit elements; how exact they have to be, the bound alone decides.
A program may use at most 64 MiB of HBM per device.

v0:
```python
import jax
import jax.numpy as jnp
from jax import lax
from jax.sharding import PartitionSpec as P

KSTEP = 4
PRECISE = lax.Precision.HIGHEST


def broadcast(block, axis, holder):
    block = jnp.where(lax.axis_index(axis) == holder, block, jnp.zeros_like(block))
    return lax.psum(block, axis)


def invert_block(diagonal):
    gram = jnp.dot(diagonal.T, diagonal, precision=PRECISE)
    factor = jnp.linalg.cholesky(gram)
    return jax.scipy.linalg.cho_solve((factor, True), diagonal.T)


def shards(front, lower_desc, upper_desc, pattern, pivot):
    rows_dev, cols_dev = front.shape
    block_size = pivot.shape[1]
    grid_rows = lax.axis_size("prow")
    grid_cols = lax.axis_size("pcol")
    own_row = lax.axis_index("prow")
    own_col = lax.axis_index("pcol")
    row_blocks = rows_dev // block_size
    col_blocks = cols_dev // block_size
    step_count = KSTEP
    layer_flags = pattern[0]
    row_flags = lax.dynamic_slice_in_dim(layer_flags, own_row * row_blocks, row_blocks)
    col_flags = lax.dynamic_slice_in_dim(
        layer_flags, row_blocks * grid_rows + own_col * col_blocks, col_blocks
    )
    row_keep = jnp.repeat(row_flags, block_size).astype(jnp.bfloat16)
    col_keep = jnp.repeat(col_flags, block_size).astype(jnp.bfloat16)
    source = (jnp.arange(row_blocks, dtype=jnp.int32)[:, None] * block_size + pivot).reshape(-1)
    lower_sorted = (lower_desc * row_keep[:, None])[source]
    upper_masked = upper_desc * col_keep[None, :]
    front_sorted = front[source].astype(jnp.float32)
    row_order = jnp.repeat(
        jnp.arange(row_blocks, dtype=jnp.int32) * grid_rows + own_row, block_size
    )
    col_order = jnp.repeat(
        jnp.arange(col_blocks, dtype=jnp.int32) * grid_cols + own_col, block_size
    )
    identity = jnp.eye(block_size, dtype=jnp.float32)
    partial_value = jnp.dot(lower_sorted, upper_masked, preferred_element_type=jnp.float32)
    panel_work = front_sorted - lax.psum(partial_value, "layer")
    for step_index in range(step_count):
        root_row = step_index % grid_rows
        root_col = step_index % grid_cols
        row_start = step_index // grid_rows * block_size
        col_start = step_index // grid_cols * block_size
        rows_below = row_order > step_index
        cols_after = col_order > step_index
        block_row = panel_work[row_start : row_start + block_size, :]
        upper_row = broadcast(block_row, "prow", root_row)
        diagonal = jnp.where(
            own_col == root_col, upper_row[:, col_start : col_start + block_size], identity
        )
        column = jnp.where(
            rows_below[:, None], panel_work[:, col_start : col_start + block_size], 0.0
        )
        lower_part = jnp.dot(column, invert_block(diagonal), precision=PRECISE)
        lower_part = broadcast(lower_part, "pcol", root_col)
        product = jnp.dot(lower_part, upper_row, precision=PRECISE)
        panel_work = panel_work - jnp.where(cols_after[None, :], product, 0.0)
        current = panel_work[:, col_start : col_start + block_size]
        placed = jnp.where(rows_below[:, None] & (own_col == root_col), lower_part, current)
        panel_work = panel_work.at[:, col_start : col_start + block_size].set(placed)
    return panel_work


def solution(mesh):
    return jax.shard_map(
        shards,
        mesh=mesh,
        in_specs=(
            P("prow", "pcol"),
            P("prow", "layer"),
            P("layer", "pcol"),
            P("layer", None),
            P("prow", None),
        ),
        out_specs=P("prow", "pcol"),
        check_vma=False,
    )
```

profile of v0, /device:TPU:0, one launch (start us, length us, event | category | flops | bytes accessed | tf_op | source)
XLA Modules:
  0.0 815.6 jit_solution(1383796101373836084)
XLA Ops:
  6.5 0.9 fusion.90
  7.6 0.7 fusion.88
  8.5 0.8 broadcast_add_fusion
  9.4 2.8 broadcast_multiply_fusion
  12.2 7.2 gather_fusion.1
  19.4 5.0 fusion.7
  24.5 5.7 gather_fusion
  30.1 169.1 %all-reduce.13.cloned.1.call-done = f32[1536,768]{1,0:T(8,128)} async-done(((f32[1536,768]{1,0:T(8,128)}), f32[1536,768]{1,0:T(8,128)}) %all-reduce.13.cloned.1.call-update) | async-done | bytes 4718608 | tf_op jit(solution)/shard_map/psum | solution.py:50
  199.2 3.6 convert_subtract_fusion
  202.8 2.2 copy-done.5
  204.9 0.8 slice_select_fusion.5
  206.4 28.6 %all-reduce.15.cloned.1.call-done = f32[192,768]{1,0:T(8,128)} async-done(((f32[192,768]{1,0:T(8,128)}), f32[192,768]{1,0:T(8,128)}) %all-reduce.15.cloned.1.call-update) | async-done | bytes 589840 | tf_op jit(solution)/shard_map/psum | solution.py:12
  235.0 1.7 fusion.31
  236.8 11.7 %cholesky.228 = f32[128,128]{1,0:T(8,128)S(1)} custom-call(f32[128,128]{1,0:T(8,128)S(1)} %cholesky.376), custom_call_target="Cholesky" | custom-call | tf_op jit(solution)/shard_map/jit(cholesky)/cholesky | solution.py:17
  248.6 9.8 %custom-call.19 = f32[1,128,128]{1,2,0:T(8,128)S(1)} custom-call(f32[1,128,128]{2,1,0:T(8,128)S(1)} %get-tuple-element.100), custom_call_target="InvertDiagBlocksLowerTriangular" | custom-call | tf_op jit(solution)/shard_map/jit(cholesky)/cholesky | solution.py:17
  258.8 5.8 cholesky.248
  267.4 20.2 %custom-call.20 = f32[2,128,128]{1,2,0:T(8,128)S(1)} custom-call(f32[2,128,128]{2,1,0:T(8,128)S(1)} %pad_maximum_fusion), custom_call_target="InvertDiagBlocksLowerTriangular" | custom-call | tf_op jit(solution)/shard_map/jit(_cho_solve)/triangular_solve | solution.py:18
  289.4 4.0 convolution_select_fusion.3
  294.3 42.2 %all-reduce.17.cloned.1.call-done = f32[1536,192]{1,0:T(8,128)} async-done(((f32[1536,192]{1,0:T(8,128)}), f32[1536,192]{1,0:T(8,128)}) %all-reduce.17.cloned.1.call-update) | async-done | bytes 1179664 | tf_op jit(solution)/shard_map/psum | solution.py:12
  336.4 7.5 select_subtract_fusion.3
  343.9 2.2 copy-done.2
  346.1 0.8 select_select_fusion.3
  346.9 8.1 scatter.14
  355.1 1.9 slice_select_fusion.4
  357.4 29.9 %all-reduce.19.cloned.1.call-done = f32[192,768]{1,0:T(8,128)} async-done(((f32[192,768]{1,0:T(8,128)}), f32[192,768]{1,0:T(8,128)}) %all-reduce.19.cloned.1.call-update) | async-done | bytes 589840 | tf_op jit(solution)/shard_map/psum | solution.py:12
  387.3 1.7 fusion.33
  389.1 11.7 %cholesky.266 = f32[128,128]{1,0:T(8,128)S(1)} custom-call(f32[128,128]{1,0:T(8,128)S(1)} %cholesky.379), custom_call_target="Cholesky" | custom-call | tf_op jit(solution)/shard_map/jit(cholesky)/cholesky | solution.py:17
  400.9 9.8 %custom-call.21 = f32[1,128,128]{1,2,0:T(8,128)S(1)} custom-call(f32[1,128,128]{2,1,0:T(8,128)S(1)} %get-tuple-element.98), custom_call_target="InvertDiagBlocksLowerTriangular" | custom-call | tf_op jit(solution)/shard_map/jit(cholesky)/cholesky | solution.py:17
  411.1 5.8 cholesky.286
  417.0 0.7 compare_reduce_fusion.4
  419.7 19.9 %custom-call.22 = f32[2,128,128]{1,2,0:T(8,128)S(1)} custom-call(f32[2,128,128]{2,1,0:T(8,128)S(1)} %pad_maximum_fusion.1), custom_call_target="InvertDiagBlocksLowerTriangular" | custom-call | tf_op jit(solution)/shard_map/jit(_cho_solve)/triangular_solve | solution.py:18
  441.4 2.6 convolution_select_fusion.2
  444.2 42.8 %all-reduce.21.cloned.1.call-done = f32[1536,192]{1,0:T(8,128)} async-done(((f32[1536,192]{1,0:T(8,128)}), f32[1536,192]{1,0:T(8,128)}) %all-reduce.21.cloned.1.call-update) | async-done | bytes 1179664 | tf_op jit(solution)/shard_map/psum | solution.py:12
  487.0 7.5 select_subtract_fusion.2
  494.5 2.2 copy-done.3
  496.7 0.8 select_select_fusion.2
  497.5 8.1 scatter.15
  505.7 1.9 slice_select_fusion.3
  508.1 29.8 %all-reduce.23.cloned.1.call-done = f32[192,768]{1,0:T(8,128)} async-done(((f32[192,768]{1,0:T(8,128)}), f32[192,768]{1,0:T(8,128)}) %all-reduce.23.cloned.1.call-update) | async-done | bytes 589840 | tf_op jit(solution)/shard_map/psum | solution.py:12
  537.9 1.7 fusion.35
  539.7 11.7 %cholesky.304 = f32[128,128]{1,0:T(8,128)S(1)} custom-call(f32[128,128]{1,0:T(8,128)S(1)} %cholesky.382), custom_call_target="Cholesky" | custom-call | tf_op jit(solution)/shard_map/jit(cholesky)/cholesky | solution.py:17
  551.5 9.8 %custom-call.23 = f32[1,128,128]{1,2,0:T(8,128)S(1)} custom-call(f32[1,128,128]{2,1,0:T(8,128)S(1)} %get-tuple-element.96), custom_call_target="InvertDiagBlocksLowerTriangular" | custom-call | tf_op jit(solution)/shard_map/jit(cholesky)/cholesky | solution.py:17
  561.7 5.8 cholesky.324
  567.5 0.7 compare_reduce_fusion.2
  570.3 20.1 %custom-call.24 = f32[2,128,128]{1,2,0:T(8,128)S(1)} custom-call(f32[2,128,128]{2,1,0:T(8,128)S(1)} %pad_maximum_fusion.2), custom_call_target="InvertDiagBlocksLowerTriangular" | custom-call | tf_op jit(solution)/shard_map/jit(_cho_solve)/triangular_solve | solution.py:18
  592.2 2.6 convolution_select_fusion.1
  595.1 42.8 %all-reduce.25.cloned.1.call-done = f32[1536,192]{1,0:T(8,128)} async-done(((f32[1536,192]{1,0:T(8,128)}), f32[1536,192]{1,0:T(8,128)}) %all-reduce.25.cloned.1.call-update) | async-done | bytes 1179664 | tf_op jit(solution)/shard_map/psum | solution.py:12
  637.8 7.5 select_subtract_fusion.1
  645.3 2.2 copy-done.4
  647.5 0.8 select_select_fusion.1
  648.3 8.1 scatter.16
  656.5 1.9 slice_select_fusion.2
  658.8 29.9 %all-reduce.27.cloned.1.call-done = f32[192,768]{1,0:T(8,128)} async-done(((f32[192,768]{1,0:T(8,128)}), f32[192,768]{1,0:T(8,128)}) %all-reduce.27.cloned.1.call-update) | async-done | bytes 589840 | tf_op jit(solution)/shard_map/psum | solution.py:12
  688.7 1.7 fusion.37
  690.5 11.7 %cholesky.342 = f32[128,128]{1,0:T(8,128)S(1)} custom-call(f32[128,128]{1,0:T(8,128)S(1)} %cholesky.385), custom_call_target="Cholesky" | custom-call | tf_op jit(solution)/shard_map/jit(cholesky)/cholesky | solution.py:17
  702.3 9.8 %custom-call.25 = f32[1,128,128]{1,2,0:T(8,128)S(1)} custom-call(f32[1,128,128]{2,1,0:T(8,128)S(1)} %get-tuple-element.94), custom_call_target="InvertDiagBlocksLowerTriangular" | custom-call | tf_op jit(solution)/shard_map/jit(cholesky)/cholesky | solution.py:17
  712.5 5.8 cholesky.362
  721.1 19.9 %custom-call.26 = f32[2,128,128]{1,2,0:T(8,128)S(1)} custom-call(f32[2,128,128]{2,1,0:T(8,128)S(1)} %pad_maximum_fusion.3), custom_call_target="InvertDiagBlocksLowerTriangular" | custom-call | tf_op jit(solution)/shard_map/jit(_cho_solve)/triangular_solve | solution.py:18
  742.8 2.6 convolution_select_fusion
  745.6 42.8 %all-reduce.29.cloned.1.call-done = f32[1536,192]{1,0:T(8,128)} async-done(((f32[1536,192]{1,0:T(8,128)}), f32[1536,192]{1,0:T(8,128)}) %all-reduce.29.cloned.1.call-update) | async-done | bytes 1179664 | tf_op jit(solution)/shard_map/psum | solution.py:12
  788.4 7.5 select_subtract_fusion
  795.9 2.2 copy-done.6
  798.1 2.1 select_select_fusion
  800.2 8.6 %scatter.19 = f32[1536,768]{1,0:T(8,128)} dynamic-update-slice(f32[1536,768]{1,0:T(8,128)} %copy-done.6, f32[1536,192]{1,0:T(8,128)} %select_select_fusion, s32[]{:T(128)} %constant.195.clone.1, s32[]{:T(128)} %constant.195.clone.1) | dynamic-update-slice | bytes 2359300 | tf_op jit(solution)/shard_map/scatter | solution.py:72
  (169 shorter events, 17.5 us)
Async XLA Ops:
  6.5 17.9 %copy-start = (bf16[1536,768]{1,0:T(8,128)(2,1)S(1)}, bf16[1536,768]{1,0:T(8,128)(2,1)}, u32[]{:S(2)}) copy-start(bf16[1536,768]{1,0:T(8,128)(2,1)} %param.16) | copy-start | bytes 7077892
  6.5 192.7 %all-reduce.13.cloned.1.call-start = ((), (), s32[]{:S(2)}) async-start(), calls=%async_computation | async-start | bytes 9437184 | tf_op jit(solution)/shard_map/psum | solution.py:50
  12.2 7.2 copy-start.15
  24.4 210.6 %all-reduce.15.cloned.1.call-start = ((), (), s32[]{:S(2)}) async-start(), calls=%async_computation.1 | async-start | bytes 1179648 | tf_op jit(solution)/shard_map/psum | solution.py:12
  202.8 2.2 copy-start.5
  205.8 130.6 %all-reduce.17.cloned.1.call-start = ((), (), s32[]{:S(2)}) async-start(), calls=%async_computation.2 | async-start | bytes 3145728 | tf_op jit(solution)/shard_map/psum | solution.py:12
  235.0 52.6 %copy-start.11 = (f32[192,768]{1,0:T(8,128)S(1)}, f32[192,768]{1,0:T(8,128)}, u32[]{:S(2)}) copy-start(f32[192,768]{1,0:T(8,128)} %all-reduce.15.cloned.1.call-done) | copy-start | bytes 1769476
  293.4 93.9 %all-reduce.19.cloned.1.call-start = ((), (), s32[]{:S(2)}) async-start(), calls=%async_computation.3 | async-start | bytes 1179648 | tf_op jit(solution)/shard_map/psum | solution.py:12
  336.4 9.7 %copy-start.7 = (f32[1536,192]{1,0:T(8,128)S(1)}, f32[1536,192]{1,0:T(8,128)}, u32[]{:S(2)}) copy-start(f32[1536,192]{1,0:T(8,128)} %all-reduce.17.cloned.1.call-done) | copy-start | bytes 3538948
  343.9 2.2 copy-start.2
  357.0 130.0 %all-reduce.21.cloned.1.call-start = ((), (), s32[]{:S(2)}) async-start(), calls=%async_computation.4 | async-start | bytes 3145728 | tf_op jit(solution)/shard_map/psum | solution.py:12
  387.3 52.3 %copy-start.13 = (f32[192,768]{1,0:T(8,128)S(1)}, f32[192,768]{1,0:T(8,128)}, u32[]{:S(2)}) copy-start(f32[192,768]{1,0:T(8,128)} %all-reduce.19.cloned.1.call-done) | copy-start | bytes 1769476
  444.0 93.8 %all-reduce.23.cloned.1.call-start = ((), (), s32[]{:S(2)}) async-start(), calls=%async_computation.5 | async-start | bytes 1179648 | tf_op jit(solution)/shard_map/psum | solution.py:12
  487.0 9.7 %copy-start.8 = (f32[1536,192]{1,0:T(8,128)S(1)}, f32[1536,192]{1,0:T(8,128)}, u32[]{:S(2)}) copy-start(f32[1536,192]{1,0:T(8,128)} %all-reduce.21.cloned.1.call-done) | copy-start | bytes 3538948
  494.5 2.2 copy-start.3
  507.6 130.2 %all-reduce.25.cloned.1.call-start = ((), (), s32[]{:S(2)}) async-start(), calls=%async_computation.6 | async-start | bytes 3145728 | tf_op jit(solution)/shard_map/psum | solution.py:12
  537.9 52.6 %copy-start.14 = (f32[192,768]{1,0:T(8,128)S(1)}, f32[192,768]{1,0:T(8,128)}, u32[]{:S(2)}) copy-start(f32[192,768]{1,0:T(8,128)} %all-reduce.23.cloned.1.call-done) | copy-start | bytes 1769476
  594.8 93.9 %all-reduce.27.cloned.1.call-start = ((), (), s32[]{:S(2)}) async-start(), calls=%async_computation.7 | async-start | bytes 1179648 | tf_op jit(solution)/shard_map/psum | solution.py:12
  637.8 9.7 %copy-start.9 = (f32[1536,192]{1,0:T(8,128)S(1)}, f32[1536,192]{1,0:T(8,128)}, u32[]{:S(2)}) copy-start(f32[1536,192]{1,0:T(8,128)} %all-reduce.25.cloned.1.call-done) | copy-start | bytes 3538948
  645.3 2.2 copy-start.4
  658.4 130.0 %all-reduce.29.cloned.1.call-start = ((), (), s32[]{:S(2)}) async-start(), calls=%async_computation.8 | async-start | bytes 3145728 | tf_op jit(solution)/shard_map/psum | solution.py:12
  688.7 52.3 %copy-start.12 = (f32[192,768]{1,0:T(8,128)S(1)}, f32[192,768]{1,0:T(8,128)}, u32[]{:S(2)}) copy-start(f32[192,768]{1,0:T(8,128)} %all-reduce.27.cloned.1.call-done) | copy-start | bytes 1769476
  788.4 9.7 %copy-start.10 = (f32[1536,192]{1,0:T(8,128)S(1)}, f32[1536,192]{1,0:T(8,128)}, u32[]{:S(2)}) copy-start(f32[1536,192]{1,0:T(8,128)} %all-reduce.29.cloned.1.call-done) | copy-start | bytes 3538948
  795.9 2.2 copy-start.6
  798.1 10.7 %copy-start.1 = (bf16[1536,768]{1,0:T(8,128)(2,1)S(1)}, bf16[1536,768]{1,0:T(8,128)(2,1)}, u32[]{:S(2)}) copy-start(bf16[1536,768]{1,0:T(8,128)(2,1)} %param.16) | copy-start | bytes 7077892
Sparse Core Ops, SparseCore 0:
  24.5 174.6 all-reduce.12
  205.9 29.0 all-reduce.14
  293.5 42.8 all-reduce.16
  357.1 30.1 all-reduce.18
  444.1 42.8 all-reduce.20
  507.7 30.0 all-reduce.22
  594.9 42.8 all-reduce.24
  658.5 30.1 all-reduce.26
  745.5 42.8 all-reduce.28
where the time goes:
time: 820 us; the launch traced here: 816 us
  waiting for transfers between devices  458 us (56%)
  other arithmetic  216 us (26%)
  matrix products  61.6 us (8%)
  local copies, waits for them, and re-layouts  59.1 us (7%)
  between operations  19.3 us (2%)
    psum x8, waiting for transfers between devices, broadcast(): return lax.psum(block, axis)  289 us
    psum x1, waiting for transfers between devices, shards(): panel_work = front_sorted - lax.psum(partial_value, 'layer')  169 us
    another operation x28, other arithmetic, invert_block(): factor = jnp.linalg.cholesky(gram)  115 us
    another operation x18, other arithmetic, invert_block(): return jax.scipy.linalg.cho_solve((factor, True), diagonal.T)  80.6 us
    scatter x4, local copies, waits for them, and re-layouts, shards(): panel_work = panel_work.at[:, col_start:col_start + block_size].set(placed)  33 us
    dot_general x4, matrix products, shards(): product = jnp.dot(lower_part, upper_row, precision=PRECISE)  29.9 us
  transfers between devices with their start and end apart: 9, of which 9 were waited for; matrix products, arithmetic and copies ran while one was open for 1% of the time, Pallas kernels for 0%

commit v1 on v0

--- a/solution.py
+++ b/solution.py
@@ -47,7 +47,7 @@
     )
     identity = jnp.eye(block_size, dtype=jnp.float32)
     partial_value = jnp.dot(lower_sorted, upper_masked, preferred_element_type=jnp.float32)
-    panel_work = front_sorted - lax.psum(partial_value, "layer")
+    panel_work = front_sorted - jnp.sum(lax.all_gather(partial_value, "layer"), axis=0)
     for step_index in range(step_count):
         root_row = step_index % grid_rows
         root_col = step_index % grid_cols

time: 820 us -> 962 us (1.17)
  waiting for transfers between devices: 458 us -> 601 us
  local copies, waits for them, and re-layouts: 59.1 us -> 45.3 us
  other arithmetic: 216 us -> 226 us
    all_gather x0 -> x1, waiting for transfers between devices: none -> 317 us  [shards(): lax.all_gather(partial_value, 'layer')]
    psum x1 -> x0, waiting for transfers between devices: 169 us -> none  [shards(): panel_work = front_sorted - lax.psum(partial_value, 'layer')]
    scatter x4 -> x1, local copies, waits for them, and re-layouts: 33 us -> 6.19 us  [shards(): panel_work = panel_work.at[:, col_start:col_start + block_size].set(placed)]
    reduce_sum x0 -> x1, other arithmetic: none -> 10.4 us  [shards(): jnp.sum(lax.all_gather(partial_value, 'layer'), axis=0)]
where the time goes in v1:
time: 962 us; the launch traced here: 956 us
  waiting for transfers between devices  601 us (62%)
  other arithmetic  226 us (23%)
  matrix products  63.3 us (7%)
  local copies, waits for them, and re-layouts  45.3 us (5%)
  between operations  19.3 us (2%)
    all_gather x1, waiting for transfers between devices, shards(): lax.all_gather(partial_value, 'layer')  317 us
    psum x8, waiting for transfers between devices, broadcast(): return lax.psum(block, axis)  284 us
    another operation x28, other arithmetic, invert_block(): factor = jnp.linalg.cholesky(gram)  115 us
    another operation x18, other arithmetic, invert_block(): return jax.scipy.linalg.cho_solve((factor, True), diagonal.T)  80.6 us
    dot_general x4, matrix products, shards(): product = jnp.dot(lower_part, upper_row, precision=PRECISE)  27.4 us
  transfers between devices with their start and end apart: 9, of which 9 were waited for; matrix products, arithmetic and copies ran while one was open for 1% of the time, Pallas kernels for 0%

profile of v1, /device:TPU:0, one launch (start us, length us, event | category | flops | bytes accessed | tf_op | source)
XLA Modules:
  0.0 955.5 jit_solution(5311723145706634508)
XLA Ops:
  6.5 0.9 fusion.94
  7.6 0.7 fusion.92
  8.5 0.8 broadcast_add_fusion
  9.4 2.8 broadcast_multiply_fusion
  12.2 7.2 gather_fusion.1
  19.4 5.0 fusion.4
  24.5 5.6 gather_fusion
  30.1 2.8 copy.12
  32.9 316.9 %all-gather.3.cloned.1.call-done = f32[6144,768]{1,0:T(8,128)} async-done(((f32[1536,768]{1,0:T(8,128)}), f32[6144,768]{1,0:T(8,128)}) %all-gather.3.cloned.1.call-update) | async-done | bytes 18874384 | tf_op jit(solution)/shard_map/all_gather | solution.py:50
  349.8 10.4 %reduce_sum.9 = f32[1536,768]{1,0:T(8,128)} reduce(f32[4,1536,768]{2,1,0:T(8,128)} %bitcast.142, f32[]{:T(128)} %constant.205.clone.1), dimensions={0}, to_apply=%region_0.0 | reduce | flops 3538944 | bytes 23592964 | tf_op jit(solution)/shard_map/reduce_sum | solution.py:50
  360.2 6.0 copy.13
  366.3 3.0 convert_subtract_fusion
  369.3 2.2 copy-done.5
  371.5 1.0 slice_select_fusion.5
  373.1 32.8 %all-reduce.12.cloned.1.call-done = f32[192,768]{0,1:T(8,128)} async-done(((f32[192,768]{0,1:T(8,128)}), f32[192,768]{0,1:T(8,128)}) %all-reduce.12.cloned.1.call-update) | async-done | bytes 589840 | tf_op jit(solution)/shard_map/psum | solution.py:12
  405.8 1.4 fusion.35
  407.4 11.7 %cholesky.228 = f32[128,128]{1,0:T(8,128)S(1)} custom-call(f32[128,128]{1,0:T(8,128)S(1)} %cholesky.376), custom_call_target="Cholesky" | custom-call | tf_op jit(solution)/shard_map/jit(cholesky)/cholesky | solution.py:17
  419.2 9.8 %custom-call.19 = f32[1,128,128]{1,2,0:T(8,128)S(1)} custom-call(f32[1,128,128]{2,1,0:T(8,128)S(1)} %get-tuple-element.100), custom_call_target="InvertDiagBlocksLowerTriangular" | custom-call | tf_op jit(solution)/shard_map/jit(cholesky)/cholesky | solution.py:17
  429.4 5.8 cholesky.248
  437.9 20.2 %custom-call.20 = f32[2,128,128]{1,2,0:T(8,128)S(1)} custom-call(f32[2,128,128]{2,1,0:T(8,128)S(1)} %pad_maximum_fusion), custom_call_target="InvertDiagBlocksLowerTriangular" | custom-call | tf_op jit(solution)/shard_map/jit(_cho_solve)/triangular_solve | solution.py:18
  460.1 3.5 convolution_select_fusion.3
  464.5 36.6 %all-reduce.14.cloned.1.call-done = f32[1536,192]{0,1:T(8,128)} async-done(((f32[1536,192]{0,1:T(8,128)}), f32[1536,192]{0,1:T(8,128)}) %all-reduce.14.cloned.1.call-update) | async-done | bytes 1179664 | tf_op jit(solution)/shard_map/psum | solution.py:12
  501.1 6.4 select_subtract_fusion.3
  507.9 1.8 copy-done.8
  509.7 1.0 fusion.15
  510.7 2.2 copy-done.2
  512.9 1.0 slice_select_fusion.4
  514.3 34.3 %all-reduce.16.cloned.1.call-done = f32[192,768]{0,1:T(8,128)} async-done(((f32[192,768]{0,1:T(8,128)}), f32[192,768]{0,1:T(8,128)}) %all-reduce.16.cloned.1.call-update) | async-done | bytes 589840 | tf_op jit(solution)/shard_map/psum | solution.py:12
  548.6 1.4 fusion.37
  550.2 11.7 %cholesky.266 = f32[128,128]{1,0:T(8,128)S(1)} custom-call(f32[128,128]{1,0:T(8,128)S(1)} %cholesky.379), custom_call_target="Cholesky" | custom-call | tf_op jit(solution)/shard_map/jit(cholesky)/cholesky | solution.py:17
  562.0 9.8 %custom-call.21 = f32[1,128,128]{1,2,0:T(8,128)S(1)} custom-call(f32[1,128,128]{2,1,0:T(8,128)S(1)} %get-tuple-element.98), custom_call_target="InvertDiagBlocksLowerTriangular" | custom-call | tf_op jit(solution)/shard_map/jit(cholesky)/cholesky | solution.py:17
  572.2 5.8 cholesky.286
  580.8 19.9 %custom-call.22 = f32[2,128,128]{1,2,0:T(8,128)S(1)} custom-call(f32[2,128,128]{2,1,0:T(8,128)S(1)} %pad_maximum_fusion.1), custom_call_target="InvertDiagBlocksLowerTriangular" | custom-call | tf_op jit(solution)/shard_map/jit(_cho_solve)/triangular_solve | solution.py:18
  602.6 4.3 convolution_select_fusion.2
  607.1 37.2 %all-reduce.18.cloned.1.call-done = f32[1536,192]{0,1:T(8,128)} async-done(((f32[1536,192]{0,1:T(8,128)}), f32[1536,192]{0,1:T(8,128)}) %all-reduce.18.cloned.1.call-update) | async-done | bytes 1179664 | tf_op jit(solution)/shard_map/psum | solution.py:12
  644.3 6.4 select_subtract_fusion.2
  651.1 1.8 copy-done.7
  652.9 1.0 fusion.16
  653.9 2.2 copy-done.3
  656.1 1.2 slice_select_fusion.3
  657.8 34.1 %all-reduce.20.cloned.1.call-done = f32[192,768]{0,1:T(8,128)} async-done(((f32[192,768]{0,1:T(8,128)}), f32[192,768]{0,1:T(8,128)}) %all-reduce.20.cloned.1.call-update) | async-done | bytes 589840 | tf_op jit(solution)/shard_map/psum | solution.py:12
  691.9 1.4 fusion.39
  693.6 11.7 %cholesky.304 = f32[128,128]{1,0:T(8,128)S(1)} custom-call(f32[128,128]{1,0:T(8,128)S(1)} %cholesky.382), custom_call_target="Cholesky" | custom-call | tf_op jit(solution)/shard_map/jit(cholesky)/cholesky | solution.py:17
  705.3 9.8 %custom-call.23 = f32[1,128,128]{1,2,0:T(8,128)S(1)} custom-call(f32[1,128,128]{2,1,0:T(8,128)S(1)} %get-tuple-element.96), custom_call_target="InvertDiagBlocksLowerTriangular" | custom-call | tf_op jit(solution)/shard_map/jit(cholesky)/cholesky | solution.py:17
  715.5 5.8 cholesky.324
  724.1 20.1 %custom-call.24 = f32[2,128,128]{1,2,0:T(8,128)S(1)} custom-call(f32[2,128,128]{2,1,0:T(8,128)S(1)} %pad_maximum_fusion.2), custom_call_target="InvertDiagBlocksLowerTriangular" | custom-call | tf_op jit(solution)/shard_map/jit(_cho_solve)/triangular_solve | solution.py:18
  746.2 4.3 convolution_select_fusion.1
  750.7 37.2 %all-reduce.22.cloned.1.call-done = f32[1536,192]{0,1:T(8,128)} async-done(((f32[1536,192]{0,1:T(8,128)}), f32[1536,192]{0,1:T(8,128)}) %all-reduce.22.cloned.1.call-update) | async-done | bytes 1179664 | tf_op jit(solution)/shard_map/psum | solution.py:12
  787.9 6.4 select_subtract_fusion.1
  794.6 1.8 copy-done.6
  796.4 1.0 fusion.17
  797.5 2.2 copy-done.4
  799.6 1.2 slice_select_fusion.2
  801.3 34.3 %all-reduce.24.cloned.1.call-done = f32[192,768]{0,1:T(8,128)} async-done(((f32[192,768]{0,1:T(8,128)}), f32[192,768]{0,1:T(8,128)}) %all-reduce.24.cloned.1.call-update) | async-done | bytes 589840 | tf_op jit(solution)/shard_map/psum | solution.py:12
  835.5 1.4 fusion.41
  837.2 11.7 %cholesky.342 = f32[128,128]{1,0:T(8,128)S(1)} custom-call(f32[128,128]{1,0:T(8,128)S(1)} %cholesky.385), custom_call_target="Cholesky" | custom-call | tf_op jit(solution)/shard_map/jit(cholesky)/cholesky | solution.py:17
  848.9 9.8 %custom-call.25 = f32[1,128,128]{1,2,0:T(8,128)S(1)} custom-call(f32[1,128,128]{2,1,0:T(8,128)S(1)} %get-tuple-element.94), custom_call_target="InvertDiagBlocksLowerTriangular" | custom-call | tf_op jit(solution)/shard_map/jit(cholesky)/cholesky | solution.py:17
  859.1 5.8 cholesky.362
  867.7 19.9 %custom-call.26 = f32[2,128,128]{1,2,0:T(8,128)S(1)} custom-call(f32[2,128,128]{2,1,0:T(8,128)S(1)} %pad_maximum_fusion.3), custom_call_target="InvertDiagBlocksLowerTriangular" | custom-call | tf_op jit(solution)/shard_map/jit(_cho_solve)/triangular_solve | solution.py:18
  889.5 4.3 convolution_select_fusion
  894.0 37.3 %all-reduce.26.cloned.1.call-done = f32[1536,192]{0,1:T(8,128)} async-done(((f32[1536,192]{0,1:T(8,128)}), f32[1536,192]{0,1:T(8,128)}) %all-reduce.26.cloned.1.call-update) | async-done | bytes 1179664 | tf_op jit(solution)/shard_map/psum | solution.py:12
  931.2 8.3 select_subtract_fusion
  939.5 3.1 fusion
  942.6 6.2 copy.18
  (176 shorter events, 20.5 us)
Async XLA Ops:
  6.5 17.9 %copy-start = (bf16[1536,768]{1,0:T(8,128)(2,1)S(1)}, bf16[1536,768]{1,0:T(8,128)(2,1)}, u32[]{:S(2)}) copy-start(bf16[1536,768]{1,0:T(8,128)(2,1)} %param.16) | copy-start | bytes 7077892
  6.5 343.3 %all-gather.3.cloned.1.call-start = ((), (), s32[]{:S(2)}) async-start(), calls=%async_computation.8 | async-start | bytes 23592960 | tf_op jit(solution)/shard_map/all_gather | solution.py:50
  12.2 7.2 copy-start.17
  24.4 381.4 %all-reduce.12.cloned.1.call-start = ((), (), s32[]{:S(2)}) async-start(), calls=%async_computation | async-start | bytes 1572864 | tf_op jit(solution)/shard_map/psum | solution.py:12
  369.3 2.2 copy-start.5
  372.5 128.6 %all-reduce.14.cloned.1.call-start = ((), (), s32[]{:S(2)}) async-start(), calls=%async_computation.1 | async-start | bytes 2359296 | tf_op jit(solution)/shard_map/psum | solution.py:12
  405.8 52.3 %copy-start.13 = (f32[192,768]{0,1:T(8,128)S(1)}, f32[192,768]{0,1:T(8,128)}, u32[]{:S(2)}) copy-start(f32[192,768]{0,1:T(8,128)} %all-reduce.12.cloned.1.call-done) | copy-start | bytes 1769476
  463.6 85.0 %all-reduce.16.cloned.1.call-start = ((), (), s32[]{:S(2)}) async-start(), calls=%async_computation.2 | async-start | bytes 1572864 | tf_op jit(solution)/shard_map/psum | solution.py:12
  507.5 2.1 copy-start.8
  507.6 2.1 copy-start.10
  510.7 2.2 copy-start.2
  513.9 130.4 %all-reduce.18.cloned.1.call-start = ((), (), s32[]{:S(2)}) async-start(), calls=%async_computation.3 | async-start | bytes 2359296 | tf_op jit(solution)/shard_map/psum | solution.py:12
  548.6 52.1 %copy-start.15 = (f32[192,768]{0,1:T(8,128)S(1)}, f32[192,768]{0,1:T(8,128)}, u32[]{:S(2)}) copy-start(f32[192,768]{0,1:T(8,128)} %all-reduce.16.cloned.1.call-done) | copy-start | bytes 1769476
  606.9 85.1 %all-reduce.20.cloned.1.call-start = ((), (), s32[]{:S(2)}) async-start(), calls=%async_computation.4 | async-start | bytes 1572864 | tf_op jit(solution)/shard_map/psum | solution.py:12
  650.7 2.1 copy-start.7
  650.7 2.1 copy-start.11
  653.9 2.2 copy-start.3
  657.3 130.6 %all-reduce.22.cloned.1.call-start = ((), (), s32[]{:S(2)}) async-start(), calls=%async_computation.5 | async-start | bytes 2359296 | tf_op jit(solution)/shard_map/psum | solution.py:12
  691.9 52.3 %copy-start.16 = (f32[192,768]{0,1:T(8,128)S(1)}, f32[192,768]{0,1:T(8,128)}, u32[]{:S(2)}) copy-start(f32[192,768]{0,1:T(8,128)} %all-reduce.20.cloned.1.call-done) | copy-start | bytes 1769476
  750.4 85.1 %all-reduce.24.cloned.1.call-start = ((), (), s32[]{:S(2)}) async-start(), calls=%async_computation.6 | async-start | bytes 1572864 | tf_op jit(solution)/shard_map/psum | solution.py:12
  794.3 2.1 copy-start.6
  794.3 2.1 copy-start.9
  797.4 2.2 copy-start.4
  800.9 130.4 %all-reduce.26.cloned.1.call-start = ((), (), s32[]{:S(2)}) async-start(), calls=%async_computation.7 | async-start | bytes 2359296 | tf_op jit(solution)/shard_map/psum | solution.py:12
  835.5 52.1 %copy-start.14 = (f32[192,768]{0,1:T(8,128)S(1)}, f32[192,768]{0,1:T(8,128)}, u32[]{:S(2)}) copy-start(f32[192,768]{0,1:T(8,128)} %all-reduce.24.cloned.1.call-done) | copy-start | bytes 1769476
  931.2 8.3 copy-start.12
  942.6 6.2 copy-start.1
Sparse Core Ops, SparseCore 0:
  24.5 325.2 all-gather.2
  372.6 33.1 all-reduce.11
  463.7 37.3 all-reduce.13
  514.1 34.5 all-reduce.15
  607.0 37.2 all-reduce.17
  657.4 34.4 all-reduce.19
  750.6 37.2 all-reduce.21
  801.0 34.5 all-reduce.23
  893.9 37.2 all-reduce.25
